TPU v7x, 512 devices: a whole 4x8x8 slice. The times are simulated.
512 devices in a mesh: doc: 16 (over x_lo, z), layer: 32 (over x_hi, y, core).
Axes of the slice: x: 4 (x_hi: 2, x_lo: 2; x = x_hi * 2 + x_lo), y: 8, z: 8, core: 2. Of those that a mesh axis runs over, the one named last changes fastest.
Arguments:
- grads: bfloat16 [8192, 32, 4096], P('doc', 'layer'), may hold values from -341 to 341
- queries: bfloat16 [1024, 32, 4096], P('doc', 'layer'), may hold values from -6 to 6
- precond: float32 [32, 4096], P('layer'), may hold values from 0.1 to 9
Outputs:
- scores: float32 [1024, 8192], P('layer', 'doc')
All inputs are finite; a program needn't handle non-finite values.
Results may differ from a plain program's by a relative error of at most 0.0029.
Values may be sent and summed in bfloat16 or wider, within the bound.
A program may use at most 64 MiB of HBM per device.

v0:
```python
import math

import jax
import jax.numpy as jnp
from jax import lax
from jax.sharding import PartitionSpec as P


def passed_along(block, axis, distance):
    devices = range(lax.axis_size(axis))
    route = [((i - distance) % len(devices), i) for i in devices]
    return lax.ppermute(block, axis, route)


def shards(grads, queries, precond):
    n_doc = lax.axis_size("doc")
    n_layer = lax.axis_size("layer")
    doc_rank = lax.axis_index("doc")
    query_dev = queries.shape[0]
    doc_dev = grads.shape[0]
    queries_all = query_dev * n_doc
    own_rows = queries_all // n_layer
    pre_queries = (queries.astype(jnp.float32) * precond[None, :, :]).astype(jnp.bfloat16)
    flat_query = pre_queries.reshape(query_dev, -1)
    flat_grads = grads.reshape(doc_dev, -1)
    doc_sq = jnp.sum(jnp.square(flat_grads.astype(jnp.float32)), axis=1)
    doc_sq = lax.psum(doc_sq, "layer")
    own_sq = jnp.sum(jnp.square(flat_query.astype(jnp.float32)), axis=1)
    placed = lax.dynamic_update_slice_in_dim(
        jnp.zeros((queries_all,), jnp.float32), own_sq, doc_rank * query_dev, 0
    )
    query_total = lax.psum(placed, ("doc", "layer"))

    def visit(carry, piece, start):
        partials, query_part = carry
        block_dots = lax.dot_general(
            piece, flat_grads, (((1,), (1,)), ((), ())), preferred_element_type=jnp.float32
        )
        partials = lax.dynamic_update_slice_in_dim(partials, block_dots, start, 0)
        block_sq = jnp.sum(jnp.square(piece.astype(jnp.float32)), axis=1)
        query_part = lax.dynamic_update_slice_in_dim(query_part, block_sq, start, 0)
        return (partials, query_part)

    initial = (
        jnp.zeros((queries_all, doc_dev), jnp.float32),
        jnp.zeros((queries_all,), jnp.float32),
    )

    def turn(step, state):
        block, totals = state
        anchor = (doc_rank - step) % n_doc
        totals = visit(totals, block, anchor * query_dev)
        block = passed_along(block, "doc", 1)
        return (block, totals)

    block, totals = lax.fori_loop(0, n_doc - 1, turn, (flat_query, initial))
    last_anchor = (doc_rank - (n_doc - 1)) % n_doc
    totals = visit(totals, block, last_anchor * query_dev)
    partials, query_part = totals
    dots = lax.psum_scatter(partials, "layer", scatter_dimension=0, tiled=True)
    query_sq = lax.dynamic_slice_in_dim(query_total, lax.axis_index("layer") * own_rows, own_rows)
    factor = math.sqrt(grads.shape[1] * n_layer * grads.shape[2])
    scores = (
        factor * dots * lax.rsqrt(query_sq + 1e-06)[:, None] * lax.rsqrt(doc_sq + 1e-06)[None, :]
    )
    return scores


def solution(mesh):
    placed = (P("doc", "layer", None), P("doc", "layer", None), P("layer", None))
    return jax.shard_map(
        shards, mesh=mesh, in_specs=placed, out_specs=P("layer", "doc"), check_vma=False
    )
```

profile of v0, /device:TPU:1, one launch (start us, length us, event | category | flops | bytes accessed | tf_op | source)
XLA Modules:
  0.0 433.6 jit_solution(1990296002809052231)
XLA Ops:
  8.1 229.7 %while.17 = (s32[]{:T(128)}, bf16[64,4096]{1,0:T(8,128)(2,1)S(1)}, f32[1024,512]{1,0:T(8,128)S(1)}, bf16[512,4096]{1,0:T(8,128)(2,1)}, s32[]{:T(128)}, /*index=5...) while((s32[]{:T(128)}, bf16[64,4096]{1,0:T(8,128)(2,1)S(1)}, ...), condition=%wide.region_1.0_spmd, body=%wide.region_0.0_spmd.sunk | while | flops 268435488 | bytes 7995712 | solution.py:56
  8.2 4.8 %collective-permute-start = (bf16[64,4096]{1,0:T(8,128)(2,1)S(1)}, bf16[64,4096]{1,0:T(8,128)(2,1)S(1)}, u32[]{:S(2)}, u32[]{:S(2)}) collective-permute-start(bf16[64,4096]{1,0:T(8,128)(2,1)S(1)} %copy.9), channel_id=1, source_target_pairs={{480,0},{0,32},{32,64},{64,96},{96,128},{128,160},{160,192},{192,2... | collective-permute-start | bytes 1572872 | tf_op jit(solution)/shard_map/while/body/eval_jaxpr/ppermute | solution.py:12
  16.6 15.6 %collective-permute-done = bf16[64,4096]{1,0:T(8,128)(2,1)S(1)} collective-permute-done((bf16[64,4096]{1,0:T(8,128)(2,1)S(1)}, bf16[64,4096]{1,0:T(8,128)(2,1)S(1)}, u32[]{:S(2)}, u32[]{:S(2)}) %collective-permute-start) | collective-permute-done | bytes 524320 | tf_op jit(solution)/shard_map/while/body/eval_jaxpr/ppermute | solution.py:12
  37.8 10.7 %collective-permute-done = bf16[64,4096]{1,0:T(8,128)(2,1)S(1)} collective-permute-done((bf16[64,4096]{1,0:T(8,128)(2,1)S(1)}, bf16[64,4096]{1,0:T(8,128)(2,1)S(1)}, u32[]{:S(2)}, u32[]{:S(2)}) %collective-permute-start) | collective-permute-done | bytes 524320 | tf_op jit(solution)/shard_map/while/body/eval_jaxpr/ppermute | solution.py:12
  54.0 9.7 %collective-permute-done = bf16[64,4096]{1,0:T(8,128)(2,1)S(1)} collective-permute-done((bf16[64,4096]{1,0:T(8,128)(2,1)S(1)}, bf16[64,4096]{1,0:T(8,128)(2,1)S(1)}, u32[]{:S(2)}, u32[]{:S(2)}) %collective-permute-start) | collective-permute-done | bytes 524320 | tf_op jit(solution)/shard_map/while/body/eval_jaxpr/ppermute | solution.py:12
  69.4 8.8 %collective-permute-done = bf16[64,4096]{1,0:T(8,128)(2,1)S(1)} collective-permute-done((bf16[64,4096]{1,0:T(8,128)(2,1)S(1)}, bf16[64,4096]{1,0:T(8,128)(2,1)S(1)}, u32[]{:S(2)}, u32[]{:S(2)}) %collective-permute-start) | collective-permute-done | bytes 524320 | tf_op jit(solution)/shard_map/while/body/eval_jaxpr/ppermute | solution.py:12
  80.2 3.6 convolution_dynamic-update-slice_fusion.3
  83.7 7.9 %collective-permute-done = bf16[64,4096]{1,0:T(8,128)(2,1)S(1)} collective-permute-done((bf16[64,4096]{1,0:T(8,128)(2,1)S(1)}, bf16[64,4096]{1,0:T(8,128)(2,1)S(1)}, u32[]{:S(2)}, u32[]{:S(2)}) %collective-permute-start) | collective-permute-done | bytes 524320 | tf_op jit(solution)/shard_map/while/body/eval_jaxpr/ppermute | solution.py:12
  93.6 3.6 convolution_dynamic-update-slice_fusion.3
  97.2 7.0 %collective-permute-done = bf16[64,4096]{1,0:T(8,128)(2,1)S(1)} collective-permute-done((bf16[64,4096]{1,0:T(8,128)(2,1)S(1)}, bf16[64,4096]{1,0:T(8,128)(2,1)S(1)}, u32[]{:S(2)}, u32[]{:S(2)}) %collective-permute-start) | collective-permute-done | bytes 524320 | tf_op jit(solution)/shard_map/while/body/eval_jaxpr/ppermute | solution.py:12
  106.2 3.6 convolution_dynamic-update-slice_fusion.3
  109.8 6.5 %collective-permute-done = bf16[64,4096]{1,0:T(8,128)(2,1)S(1)} collective-permute-done((bf16[64,4096]{1,0:T(8,128)(2,1)S(1)}, bf16[64,4096]{1,0:T(8,128)(2,1)S(1)}, u32[]{:S(2)}, u32[]{:S(2)}) %collective-permute-start) | collective-permute-done | bytes 524320 | tf_op jit(solution)/shard_map/while/body/eval_jaxpr/ppermute | solution.py:12
  121.8 6.5 %collective-permute-done = bf16[64,4096]{1,0:T(8,128)(2,1)S(1)} collective-permute-done((bf16[64,4096]{1,0:T(8,128)(2,1)S(1)}, bf16[64,4096]{1,0:T(8,128)(2,1)S(1)}, u32[]{:S(2)}, u32[]{:S(2)}) %collective-permute-start) | collective-permute-done | bytes 524320 | tf_op jit(solution)/shard_map/while/body/eval_jaxpr/ppermute | solution.py:12
  133.9 7.5 %collective-permute-done = bf16[64,4096]{1,0:T(8,128)(2,1)S(1)} collective-permute-done((bf16[64,4096]{1,0:T(8,128)(2,1)S(1)}, bf16[64,4096]{1,0:T(8,128)(2,1)S(1)}, u32[]{:S(2)}, u32[]{:S(2)}) %collective-permute-start) | collective-permute-done | bytes 524320 | tf_op jit(solution)/shard_map/while/body/eval_jaxpr/ppermute | solution.py:12
  147.0 8.6 %collective-permute-done = bf16[64,4096]{1,0:T(8,128)(2,1)S(1)} collective-permute-done((bf16[64,4096]{1,0:T(8,128)(2,1)S(1)}, bf16[64,4096]{1,0:T(8,128)(2,1)S(1)}, u32[]{:S(2)}, u32[]{:S(2)}) %collective-permute-start) | collective-permute-done | bytes 524320 | tf_op jit(solution)/shard_map/while/body/eval_jaxpr/ppermute | solution.py:12
  161.1 9.7 %collective-permute-done = bf16[64,4096]{1,0:T(8,128)(2,1)S(1)} collective-permute-done((bf16[64,4096]{1,0:T(8,128)(2,1)S(1)}, bf16[64,4096]{1,0:T(8,128)(2,1)S(1)}, u32[]{:S(2)}, u32[]{:S(2)}) %collective-permute-start) | collective-permute-done | bytes 524320 | tf_op jit(solution)/shard_map/while/body/eval_jaxpr/ppermute | solution.py:12
  176.3 10.7 %collective-permute-done = bf16[64,4096]{1,0:T(8,128)(2,1)S(1)} collective-permute-done((bf16[64,4096]{1,0:T(8,128)(2,1)S(1)}, bf16[64,4096]{1,0:T(8,128)(2,1)S(1)}, u32[]{:S(2)}, u32[]{:S(2)}) %collective-permute-start) | collective-permute-done | bytes 524320 | tf_op jit(solution)/shard_map/while/body/eval_jaxpr/ppermute | solution.py:12
  189.1 3.6 convolution_dynamic-update-slice_fusion.3
  192.6 11.8 %collective-permute-done = bf16[64,4096]{1,0:T(8,128)(2,1)S(1)} collective-permute-done((bf16[64,4096]{1,0:T(8,128)(2,1)S(1)}, bf16[64,4096]{1,0:T(8,128)(2,1)S(1)}, u32[]{:S(2)}, u32[]{:S(2)}) %collective-permute-start) | collective-permute-done | bytes 524320 | tf_op jit(solution)/shard_map/while/body/eval_jaxpr/ppermute | solution.py:12
  206.5 3.6 convolution_dynamic-update-slice_fusion.3
  210.1 11.6 %collective-permute-done = bf16[64,4096]{1,0:T(8,128)(2,1)S(1)} collective-permute-done((bf16[64,4096]{1,0:T(8,128)(2,1)S(1)}, bf16[64,4096]{1,0:T(8,128)(2,1)S(1)}, u32[]{:S(2)}, u32[]{:S(2)}) %collective-permute-start) | collective-permute-done | bytes 524320 | tf_op jit(solution)/shard_map/while/body/eval_jaxpr/ppermute | solution.py:12
  227.2 10.7 %collective-permute-done = bf16[64,4096]{1,0:T(8,128)(2,1)S(1)} collective-permute-done((bf16[64,4096]{1,0:T(8,128)(2,1)S(1)}, bf16[64,4096]{1,0:T(8,128)(2,1)S(1)}, u32[]{:S(2)}, u32[]{:S(2)}) %collective-permute-start) | collective-permute-done | bytes 524320 | tf_op jit(solution)/shard_map/while/body/eval_jaxpr/ppermute | solution.py:12
  243.1 113.9 %psum.14 = f32[1024]{0:T(1024)S(1)} all-reduce(f32[1024]{0:T(1024)S(1)} %dynamic_update_slice.17), channel_id=1, replica_groups=mesh['doc'=16,'layer'=32] {'doc','layer'}, use_global_device_ids=true, to_apply=%region_4.5 | all-reduce | flops 1024 | bytes 8192 | tf_op jit(solution)/shard_map/psum | solution.py:32
  360.1 65.0 %psum.15 = f32[512]{0:T(512)S(1)} all-reduce(f32[512]{0:T(512)S(1)} %multiply_reduce_fusion), channel_id=1, replica_groups=mesh['doc'=16,'layer'=32] {'layer'}, use_global_device_ids=true, to_apply=%region_6.7 | all-reduce | flops 512 | bytes 4096 | tf_op jit(solution)/shard_map/psum | solution.py:27
  (53 shorter events, 74.7 us)
Async XLA Ops:
  6.5 418.6 %reduce-scatter.2.cloned.1.call-start = ((), (), s32[]{:S(2)}) async-start(), calls=%async_computation.1 | async-start | bytes 2162688 | tf_op jit(solution)/shard_map/reduce_scatter | solution.py:60
  8.2 24.1 %collective-permute-start = (bf16[64,4096]{1,0:T(8,128)(2,1)S(1)}, bf16[64,4096]{1,0:T(8,128)(2,1)S(1)}, u32[]{:S(2)}, u32[]{:S(2)}) collective-permute-start(bf16[64,4096]{1,0:T(8,128)(2,1)S(1)} %copy.9), channel_id=1, source_target_pairs={{480,0},{0,32},{32,64},{64,96},{96,128},{128,160},{160,192},{192,2... | collective-permute-start | bytes 1572872 | tf_op jit(solution)/shard_map/while/body/eval_jaxpr/ppermute | solution.py:12
  32.3 16.2 %collective-permute-start = (bf16[64,4096]{1,0:T(8,128)(2,1)S(1)}, bf16[64,4096]{1,0:T(8,128)(2,1)S(1)}, u32[]{:S(2)}, u32[]{:S(2)}) collective-permute-start(bf16[64,4096]{1,0:T(8,128)(2,1)S(1)} %copy.9), channel_id=1, source_target_pairs={{480,0},{0,32},{32,64},{64,96},{96,128},{128,160},{160,192},{192,2... | collective-permute-start | bytes 1572872 | tf_op jit(solution)/shard_map/while/body/eval_jaxpr/ppermute | solution.py:12
  48.5 15.3 %collective-permute-start = (bf16[64,4096]{1,0:T(8,128)(2,1)S(1)}, bf16[64,4096]{1,0:T(8,128)(2,1)S(1)}, u32[]{:S(2)}, u32[]{:S(2)}) collective-permute-start(bf16[64,4096]{1,0:T(8,128)(2,1)S(1)} %copy.9), channel_id=1, source_target_pairs={{480,0},{0,32},{32,64},{64,96},{96,128},{128,160},{160,192},{192,2... | collective-permute-start | bytes 1572872 | tf_op jit(solution)/shard_map/while/body/eval_jaxpr/ppermute | solution.py:12
  63.8 14.3 %collective-permute-start = (bf16[64,4096]{1,0:T(8,128)(2,1)S(1)}, bf16[64,4096]{1,0:T(8,128)(2,1)S(1)}, u32[]{:S(2)}, u32[]{:S(2)}) collective-permute-start(bf16[64,4096]{1,0:T(8,128)(2,1)S(1)} %copy.9), channel_id=1, source_target_pairs={{480,0},{0,32},{32,64},{64,96},{96,128},{128,160},{160,192},{192,2... | collective-permute-start | bytes 1572872 | tf_op jit(solution)/shard_map/while/body/eval_jaxpr/ppermute | solution.py:12
  78.2 13.4 %collective-permute-start = (bf16[64,4096]{1,0:T(8,128)(2,1)S(1)}, bf16[64,4096]{1,0:T(8,128)(2,1)S(1)}, u32[]{:S(2)}, u32[]{:S(2)}) collective-permute-start(bf16[64,4096]{1,0:T(8,128)(2,1)S(1)} %copy.9), channel_id=1, source_target_pairs={{480,0},{0,32},{32,64},{64,96},{96,128},{128,160},{160,192},{192,2... | collective-permute-start | bytes 1572872 | tf_op jit(solution)/shard_map/while/body/eval_jaxpr/ppermute | solution.py:12
  91.7 12.5 %collective-permute-start = (bf16[64,4096]{1,0:T(8,128)(2,1)S(1)}, bf16[64,4096]{1,0:T(8,128)(2,1)S(1)}, u32[]{:S(2)}, u32[]{:S(2)}) collective-permute-start(bf16[64,4096]{1,0:T(8,128)(2,1)S(1)} %copy.9), channel_id=1, source_target_pairs={{480,0},{0,32},{32,64},{64,96},{96,128},{128,160},{160,192},{192,2... | collective-permute-start | bytes 1572872 | tf_op jit(solution)/shard_map/while/body/eval_jaxpr/ppermute | solution.py:12
  104.2 12.0 %collective-permute-start = (bf16[64,4096]{1,0:T(8,128)(2,1)S(1)}, bf16[64,4096]{1,0:T(8,128)(2,1)S(1)}, u32[]{:S(2)}, u32[]{:S(2)}) collective-permute-start(bf16[64,4096]{1,0:T(8,128)(2,1)S(1)} %copy.9), channel_id=1, source_target_pairs={{480,0},{0,32},{32,64},{64,96},{96,128},{128,160},{160,192},{192,2... | collective-permute-start | bytes 1572872 | tf_op jit(solution)/shard_map/while/body/eval_jaxpr/ppermute | solution.py:12
  116.3 12.0 %collective-permute-start = (bf16[64,4096]{1,0:T(8,128)(2,1)S(1)}, bf16[64,4096]{1,0:T(8,128)(2,1)S(1)}, u32[]{:S(2)}, u32[]{:S(2)}) collective-permute-start(bf16[64,4096]{1,0:T(8,128)(2,1)S(1)} %copy.9), channel_id=1, source_target_pairs={{480,0},{0,32},{32,64},{64,96},{96,128},{128,160},{160,192},{192,2... | collective-permute-start | bytes 1572872 | tf_op jit(solution)/shard_map/while/body/eval_jaxpr/ppermute | solution.py:12
  128.4 13.0 %collective-permute-start = (bf16[64,4096]{1,0:T(8,128)(2,1)S(1)}, bf16[64,4096]{1,0:T(8,128)(2,1)S(1)}, u32[]{:S(2)}, u32[]{:S(2)}) collective-permute-start(bf16[64,4096]{1,0:T(8,128)(2,1)S(1)} %copy.9), channel_id=1, source_target_pairs={{480,0},{0,32},{32,64},{64,96},{96,128},{128,160},{160,192},{192,2... | collective-permute-start | bytes 1572872 | tf_op jit(solution)/shard_map/while/body/eval_jaxpr/ppermute | solution.py:12
  141.4 14.1 %collective-permute-start = (bf16[64,4096]{1,0:T(8,128)(2,1)S(1)}, bf16[64,4096]{1,0:T(8,128)(2,1)S(1)}, u32[]{:S(2)}, u32[]{:S(2)}) collective-permute-start(bf16[64,4096]{1,0:T(8,128)(2,1)S(1)} %copy.9), channel_id=1, source_target_pairs={{480,0},{0,32},{32,64},{64,96},{96,128},{128,160},{160,192},{192,2... | collective-permute-start | bytes 1572872 | tf_op jit(solution)/shard_map/while/body/eval_jaxpr/ppermute | solution.py:12
  155.6 15.2 %collective-permute-start = (bf16[64,4096]{1,0:T(8,128)(2,1)S(1)}, bf16[64,4096]{1,0:T(8,128)(2,1)S(1)}, u32[]{:S(2)}, u32[]{:S(2)}) collective-permute-start(bf16[64,4096]{1,0:T(8,128)(2,1)S(1)} %copy.9), channel_id=1, source_target_pairs={{480,0},{0,32},{32,64},{64,96},{96,128},{128,160},{160,192},{192,2... | collective-permute-start | bytes 1572872 | tf_op jit(solution)/shard_map/while/body/eval_jaxpr/ppermute | solution.py:12
  170.8 16.3 %collective-permute-start = (bf16[64,4096]{1,0:T(8,128)(2,1)S(1)}, bf16[64,4096]{1,0:T(8,128)(2,1)S(1)}, u32[]{:S(2)}, u32[]{:S(2)}) collective-permute-start(bf16[64,4096]{1,0:T(8,128)(2,1)S(1)} %copy.9), channel_id=1, source_target_pairs={{480,0},{0,32},{32,64},{64,96},{96,128},{128,160},{160,192},{192,2... | collective-permute-start | bytes 1572872 | tf_op jit(solution)/shard_map/while/body/eval_jaxpr/ppermute | solution.py:12
  187.1 17.4 %collective-permute-start = (bf16[64,4096]{1,0:T(8,128)(2,1)S(1)}, bf16[64,4096]{1,0:T(8,128)(2,1)S(1)}, u32[]{:S(2)}, u32[]{:S(2)}) collective-permute-start(bf16[64,4096]{1,0:T(8,128)(2,1)S(1)} %copy.9), channel_id=1, source_target_pairs={{480,0},{0,32},{32,64},{64,96},{96,128},{128,160},{160,192},{192,2... | collective-permute-start | bytes 1572872 | tf_op jit(solution)/shard_map/while/body/eval_jaxpr/ppermute | solution.py:12
  204.5 17.1 %collective-permute-start = (bf16[64,4096]{1,0:T(8,128)(2,1)S(1)}, bf16[64,4096]{1,0:T(8,128)(2,1)S(1)}, u32[]{:S(2)}, u32[]{:S(2)}) collective-permute-start(bf16[64,4096]{1,0:T(8,128)(2,1)S(1)} %copy.9), channel_id=1, source_target_pairs={{480,0},{0,32},{32,64},{64,96},{96,128},{128,160},{160,192},{192,2... | collective-permute-start | bytes 1572872 | tf_op jit(solution)/shard_map/while/body/eval_jaxpr/ppermute | solution.py:12
  221.7 16.2 %collective-permute-start = (bf16[64,4096]{1,0:T(8,128)(2,1)S(1)}, bf16[64,4096]{1,0:T(8,128)(2,1)S(1)}, u32[]{:S(2)}, u32[]{:S(2)}) collective-permute-start(bf16[64,4096]{1,0:T(8,128)(2,1)S(1)} %copy.9), channel_id=1, source_target_pairs={{480,0},{0,32},{32,64},{64,96},{96,128},{128,160},{160,192},{192,2... | collective-permute-start | bytes 1572872 | tf_op jit(solution)/shard_map/while/body/eval_jaxpr/ppermute | solution.py:12
  241.4 1.4 copy-start
Sparse Core Ops, SparseCore 0:
  242.9 133.3 reduce-scatter.1
where the time goes:
time: 435 us; the launch traced here: 434 us
  blocking collectives  179 us (41%)
  waiting for transfers between devices  143 us (33%)
  matrix products  57.3 us (13%)
  starting transfers between devices  31.7 us (7%)
  between operations  13.4 us (3%)
  other arithmetic  6.04 us (1%)
    ppermute x15, waiting for transfers between devices, passed_along(): return lax.ppermute(block, axis, route)  143 us
    psum x1, blocking collectives, shards(): query_total = lax.psum(placed, ('doc', 'layer'))  114 us
    psum x1, blocking collectives, shards(): doc_sq = lax.psum(doc_sq, 'layer')  65 us
    dot_general x16, matrix products, visit(): lax.dot_general(piece, flat_grads, (((1,), (1,)), ((), ())), preferred_el...  57.3 us
    ppermute x15, starting transfers between devices, passed_along(): return lax.ppermute(block, axis, route)  31.7 us
  transfers between devices with their start and end apart: 16, of which 15 were waited for; matrix products, arithmetic and copies ran while one was open for 13% of the time, Pallas kernels for 0%

commit v1 on v0

v1 whole, which is shorter than its diff:
```python
import functools
import math

import jax
import jax.numpy as jnp
from jax import lax
from jax.experimental import pallas as pl
from jax.experimental.pallas import tpu as pltpu
from jax.sharding import PartitionSpec as P

MESH = pl.DeviceIdType.MESH
NT = (((1,), (1,)), ((), ()))
CHUNK = 16
EXTRA = 128

SLOTS = (
    (0, 0), (0, -1), (0, 1), (1, 0), (0, -2), (0, 2), (0, -3), (0, 3),
    (0, 4), (1, -3), (1, 3), (1, -1), (1, 1), (1, -2), (1, 2), (1, 4),
)


def kernel(
    n_doc, n_layer, factor,
    g_hbm, q_ref, pc_ref, out_ref,
    g, gath, part, cx, rs_out, rs_in, ds_part, ds_cx, ds_out, ds_in,
    g_sem, ag_send, ag_recv, cx_send, cx_recv, rs_send, rs_recv, dsc_send, dsc_recv, ds_send, ds_recv,
):
    n_z = n_doc // 2
    chips = n_layer // 2
    docs, width = g.shape
    rows = q_ref.shape[0]
    half = rows // 2
    n_chunks = rows // CHUNK
    mid = n_chunks // 2
    doc = lax.axis_index("doc")
    layer = lax.axis_index("layer")
    col = doc // n_z
    z = lax.rem(doc, n_z)
    chip = layer // 2
    core = lax.rem(layer, 2)

    def doc_at(other, dz):
        c = (1 - col) if other else col
        return c * n_z + lax.rem(z + (dz + n_z), n_z)

    up = (doc_at(0, 1), layer)
    down = (doc_at(0, -1), layer)
    across = (doc_at(1, 0), layer)
    twin = (doc, 2 * chip + 1 - core)

    def chip_dev(c):
        return (doc, 2 * c + core)

    barrier = pltpu.get_barrier_semaphore()
    for dev in (up, down, across, twin):
        pl.semaphore_signal(barrier, inc=1, device_id=dev, device_id_type=MESH)

    def greet(k, carry):
        pl.semaphore_signal(barrier, inc=1, device_id=chip_dev(lax.rem(chip + k, chips)), device_id_type=MESH)
        return carry

    lax.fori_loop(1, chips, greet, 0)

    load = pltpu.make_async_copy(g_hbm, g, g_sem)
    load.start()
    gath[0] = (q_ref[...].astype(jnp.float32) * pc_ref[...]).astype(jnp.bfloat16)
    pl.semaphore_wait(barrier, 4 + chips - 1)

    def piece(slot, c):
        return gath.at[slot, pl.ds(c * CHUNK, CHUNK), :]

    def send(src, dst, c, dev):
        pltpu.make_async_remote_copy(
            src_ref=piece(src, c), dst_ref=piece(dst, c), send_sem=ag_send, recv_sem=ag_recv.at[dst, c],
            device_id=dev, device_id_type=MESH,
        ).start()

    def arrived(slot, c):
        pltpu.make_async_copy(piece(slot, c), piece(slot, c), ag_recv.at[slot, c]).wait()

    def multiply(first, last):
        n = last - first
        x = gath[first:last].reshape(n * rows, width)
        dots = lax.dot_general(x, g[...], NT, preferred_element_type=jnp.float32)
        part[first:last, :, :, :docs] = dots.reshape(n, 2, half, docs)
        for s in range(first, last):
            v = gath[s].astype(jnp.float32)
            sq = jnp.sum(v * v, axis=1, keepdims=True)
            part[s, :, :, docs:] = jnp.broadcast_to(sq, (rows, EXTRA)).reshape(2, half, EXTRA)
        for s in range(first, last):
            pltpu.make_async_remote_copy(
                src_ref=part.at[s, 1 - core], dst_ref=cx.at[s], send_sem=cx_send, recv_sem=cx_recv.at[s],
                device_id=twin, device_id_type=MESH,
            ).start()

    def reduce_out(first, last):
        for s in range(first, last):
            pltpu.make_async_copy(cx.at[s], cx.at[s], cx_recv.at[s]).wait()
            v = part[s, core] + cx[s]
            dots = v[:, :docs].astype(jnp.bfloat16)
            sq = v[:, docs:]
            high = sq.astype(jnp.bfloat16)
            low = (sq - high.astype(jnp.float32)).astype(jnp.bfloat16)
            lane = lax.broadcasted_iota(jnp.int32, sq.shape, 1)
            both = jnp.where(lane < EXTRA // 2, high.astype(jnp.float32), low.astype(jnp.float32))
            rs_out[s, :, :docs] = dots
            rs_out[s, :, docs:] = both.astype(jnp.bfloat16)
            owner = doc_at(*SLOTS[s])

            @pl.when(owner != chip)
            def _():
                pltpu.make_async_remote_copy(
                    src_ref=rs_out.at[s], dst_ref=rs_in.at[chip], send_sem=rs_send, recv_sem=rs_recv,
                    device_id=chip_dev(owner), device_id_type=MESH,
                ).start()

            @pl.when(owner == chip)
            def _():
                rs_in[chip] = rs_out[s]

    chunks = range(n_chunks)
    for c in chunks:
        send(0, 1, c, up)
        send(0, 2, c, down)
        send(0, 3, c, across)

    load.wait()
    sq_rows = 64
    acc_rows = []
    for i in range(docs // sq_rows):
        acc = jnp.zeros((sq_rows, 128), jnp.float32)
        for k in range(width // 128):
            v = g[i * sq_rows : (i + 1) * sq_rows, k * 128 : (k + 1) * 128].astype(jnp.float32)
            acc = acc + v * v
        acc_rows.append(acc)
    lanes = jnp.concatenate(acc_rows, axis=0)
    ones = jnp.ones((8, 128), jnp.float32)
    doc_sq = lax.dot_general(ones, lanes, NT, preferred_element_type=jnp.float32, precision=lax.Precision.HIGHEST)
    ds_part[...] = doc_sq[0:1]
    pltpu.make_async_remote_copy(
        src_ref=ds_part, dst_ref=ds_cx, send_sem=dsc_send, recv_sem=dsc_recv, device_id=twin, device_id_type=MESH
    ).start()

    for c in chunks:
        arrived(1, c)
        send(1, 4, c, up)
        arrived(2, c)
        send(2, 5, c, down)
    for c in chunks:
        arrived(3, c)
    multiply(0, 4)

    pltpu.make_async_copy(ds_cx, ds_cx, dsc_recv).wait()
    ds_out[...] = ds_part[...] + ds_cx[...]
    ds_in[chip] = ds_out[...]

    def spread(k, carry):
        pltpu.make_async_remote_copy(
            src_ref=ds_out, dst_ref=ds_in.at[chip], send_sem=ds_send, recv_sem=ds_recv,
            device_id=chip_dev(lax.rem(chip + k, chips)), device_id_type=MESH,
        ).start()
        return carry

    lax.fori_loop(1, chips, spread, 0)

    for c in chunks:
        arrived(4, c)
        send(4, 6, c, up)
        arrived(5, c)
        send(5, 7, c, down)
        if c < mid:
            send(4, 13, c, across)
            send(5, 14, c, across)
    multiply(4, 6)
    reduce_out(0, 4)

    for c in chunks:
        arrived(6, c)
        if c < mid:
            send(6, 8, c, up)
        send(6, 9, c, across)
        arrived(7, c)
        if c >= mid:
            send(7, 8, c, down)
        send(7, 10, c, across)
    late = tuple(range(mid, n_chunks))
    early = tuple(range(mid))
    for c in late + early:
        send(3, 11, c, up)
        send(3, 12, c, down)
    multiply(6, 8)
    reduce_out(4, 6)

    for c in chunks:
        arrived(8, c)
        send(8, 15, c, across)
    for c in late:
        arrived(11, c)
        send(11, 13, c, up)
        arrived(12, c)
        send(12, 14, c, down)
    for c in chunks:
        arrived(9, c)
        arrived(10, c)
    multiply(8, 11)
    reduce_out(6, 8)
    for c in early:
        arrived(11, c)
        arrived(12, c)
    multiply(11, 13)
    reduce_out(8, 11)
    for c in chunks:
        arrived(13, c)
        arrived(14, c)
        arrived(15, c)
    multiply(13, 16)
    reduce_out(11, 13)
    reduce_out(13, 16)

    def taken(ref, sem):
        pltpu.make_async_copy(ref, ref, sem).wait()

    taken(ds_in.at[pl.ds(0, chips - 1)], ds_recv)
    doc_total = jnp.sum(ds_in[...], axis=0)
    taken(rs_in.at[pl.ds(0, chips - 1)], rs_recv)
    total = rs_in[0].astype(jnp.float32)
    for k in range(1, chips):
        total = total + rs_in[k].astype(jnp.float32)
    query_sq = total[:, docs : docs + 1] + total[:, docs + EXTRA // 2 : docs + EXTRA // 2 + 1]
    out_ref[...] = (
        factor * total[:, :docs] * lax.rsqrt(query_sq + 1e-06) * lax.rsqrt(doc_total + 1e-06)
    )

    taken(gath.at[pl.ds(0, n_doc - 1)], ag_send)
    taken(cx, cx_send)
    taken(rs_out.at[pl.ds(0, chips - 1)], rs_send)
    taken(ds_cx, dsc_send)
    taken(ds_in.at[pl.ds(0, chips - 1)], ds_send)


def shards(grads, queries, precond):
    n_doc = lax.axis_size("doc")
    n_layer = lax.axis_size("layer")
    docs, width = grads.shape[0], grads.shape[2]
    rows = queries.shape[0]
    half = rows // 2
    chips = n_layer // 2
    own_rows = rows * n_doc // n_layer
    factor = math.sqrt(n_layer * width)
    dma = pltpu.SemaphoreType.DMA
    return pl.pallas_call(
        functools.partial(kernel, n_doc, n_layer, factor),
        out_shape=jax.ShapeDtypeStruct((own_rows, docs), jnp.float32),
        in_specs=[
            pl.BlockSpec(memory_space=pl.ANY),
            pl.BlockSpec(memory_space=pltpu.VMEM),
            pl.BlockSpec(memory_space=pltpu.VMEM),
        ],
        out_specs=pl.BlockSpec(memory_space=pltpu.VMEM),
        scratch_shapes=[
            pltpu.VMEM((docs, width), jnp.bfloat16),
            pltpu.VMEM((n_doc, rows, width), jnp.bfloat16),
            pltpu.VMEM((n_doc, 2, half, docs + EXTRA), jnp.float32),
            pltpu.VMEM((n_doc, half, docs + EXTRA), jnp.float32),
            pltpu.VMEM((n_doc, half, docs + EXTRA), jnp.bfloat16),
            pltpu.VMEM((chips, half, docs + EXTRA), jnp.bfloat16),
            pltpu.VMEM((1, docs), jnp.float32),
            pltpu.VMEM((1, docs), jnp.float32),
            pltpu.VMEM((1, docs), jnp.float32),
            pltpu.VMEM((chips, 1, docs), jnp.float32),
            dma, dma, dma((n_doc, rows // CHUNK)), dma, dma((n_doc,)), dma, dma, dma, dma, dma, dma,
        ],
        compiler_params=pltpu.CompilerParams(
            collective_id=0, has_side_effects=True, vmem_limit_bytes=48 << 20
        ),
        cost_estimate=pl.CostEstimate(
            flops=2 * rows * n_doc * docs * width, bytes_accessed=2 * docs * width, transcendentals=0
        ),
        name="gather_multiply_reduce",
    )(grads.reshape(docs, width), queries.reshape(rows, width), precond)


def solution(mesh):
    placed = (P("doc", "layer", None), P("doc", "layer", None), P("layer", None))
    return jax.shard_map(
        shards, mesh=mesh, in_specs=placed, out_specs=P("layer", "doc"), check_vma=False
    )
```

time: 435 us -> 100 us (0.23)
  blocking collectives: 179 us -> 0 us
  waiting for transfers between devices: 143 us -> 0 us
  Pallas kernels: 0 us -> 95.3 us
  matrix products: 57.3 us -> 0 us
  starting transfers between devices: 31.7 us -> 0 us
  between operations: 13.4 us -> 0.01 us
  other arithmetic: 6.04 us -> 0 us
    psum x2 -> x0, blocking collectives: 179 us -> none  [the longest x1 114 us: shards(): query_total = lax.psum(placed, ('doc', 'layer'))]
    ppermute x15 -> x0, waiting for transfers between devices: 143 us -> none  [passed_along(): return lax.ppermute(block, axis, route)]
    pallas_call x0 -> x1, Pallas kernels: none -> 95.3 us  [shards(): pl.pallas_call(functools.partial(kernel, n_doc, n_layer, factor), out_sha...]
    dot_general x16 -> x0, matrix products: 57.3 us -> none  [visit(): lax.dot_general(piece, flat_grads, (((1,), (1,)), ((), ())), preferred_el...]
    ppermute x15 -> x0, starting transfers between devices: 31.7 us -> none  [passed_along(): return lax.ppermute(block, axis, route)]
    reduce_sum x2 -> x0, other arithmetic: 4.41 us -> none  [the longest x1 3.1 us: shards(): doc_sq = jnp.sum(jnp.square(flat_grads.astype(jnp.float32)), axis=1)]
  transfers between devices with their start and end apart: 16 -> 0, of which waited for: 15 -> 0; matrix products, arithmetic and copies ran while one was open for 13% -> 0% of each run, Pallas kernels for 0% -> 0%
where the time goes in v1:
time: 100 us; the launch traced here: 99.9 us
  Pallas kernels  95.3 us (95%)
  local copies, waits for them, and re-layouts  4.58 us (5%)
    pallas_call x1, Pallas kernels, shards(): pl.pallas_call(functools.partial(kernel, n_doc, n_layer, factor), out_sha...  95.3 us
    unnamed x7, local copies, waits for them, and re-layouts  4.58 us

profile of v1, /device:TPU:1, one launch (start us, length us, event | category | flops | bytes accessed | tf_op | source)
XLA Modules:
  0.0 99.9 jit_solution(6462492493044868717)
XLA Ops:
  0.0 0.0 copy-start
  0.0 2.2 %copy-done = bf16[512,1,4096]{2,0,1:T(8,128)(2,1)S(1)} copy-done((bf16[512,1,4096]{2,0,1:T(8,128)(2,1)S(1)}, bf16[512,1,4096]{2,0,1:T(8,128)(2,1)}, u32[]{:S(2)}) %copy-start) | copy-done | bytes 4194328
  2.2 0.0 copy-start.1
  2.2 1.0 %copy-done.1 = bf16[64,1,4096]{2,0,1:T(8,128)(2,1)S(1)} copy-done((bf16[64,1,4096]{2,0,1:T(8,128)(2,1)S(1)}, bf16[64,1,4096]{2,0,1:T(8,128)(2,1)}, u32[]{:S(2)}) %copy-start.1) | copy-done | bytes 524312
  3.2 0.0 copy-start.2
  3.2 0.7 copy-done.2
  3.9 95.3 %gather_multiply_reduce.1 = f32[32,512]{1,0:T(8,128)S(1)} custom-call(bf16[512,4096]{1,0:T(8,128)(2,1)S(1)} %bitcast.2, bf16[64,4096]{1,0:T(8,128)(2,1)S(1)} %bitcast.3, f32[1,4096]{1,0:T(1,128)S(1)} %copy-done.2), custom_call_target="tpu_custom_call" | custom-call | flops 4294967296 | bytes 4194304 | tf_op jit(solution)/shard_map/gather_multiply_reduce/pallas_call | solution.py:251
  99.3 0.6 copy.5
Async XLA Ops:
  0.0 2.2 %copy-start = (bf16[512,1,4096]{2,0,1:T(8,128)(2,1)S(1)}, bf16[512,1,4096]{2,0,1:T(8,128)(2,1)}, u32[]{:S(2)}) copy-start(bf16[512,1,4096]{2,0,1:T(8,128)(2,1)} %param.3) | copy-start | bytes 12582916
  2.2 1.0 %copy-start.1 = (bf16[64,1,4096]{2,0,1:T(8,128)(2,1)S(1)}, bf16[64,1,4096]{2,0,1:T(8,128)(2,1)}, u32[]{:S(2)}) copy-start(bf16[64,1,4096]{2,0,1:T(8,128)(2,1)} %param.4) | copy-start | bytes 1572868
  3.2 0.7 copy-start.2

commit v2 on v0

v2 whole, which is shorter than its diff:
```python
import functools
import math

import jax
import jax.numpy as jnp
from jax import lax
from jax.experimental import pallas as pl
from jax.experimental.pallas import tpu as pltpu
from jax.sharding import PartitionSpec as P

MESH = pl.DeviceIdType.MESH
NT = (((1,), (1,)), ((), ()))
F32 = jnp.float32
BF16 = jnp.bfloat16

OFFSETS = (0, -1, 1, -2, 2, -3, 3, 4)
UP = (1, 3, 5, 7)
DOWN = (2, 4, 6, 7)
EXTRA = 128
PIECES = 4


def kernel(
    n_doc, n_layer, swap, factor,
    g_hbm, q_hbm, pc_hbm, out_ref,
    g_own, g_send, g_oth, q_own, q_oth, pc_own, pc_oth, gath, px, part, cx, rs_out, rs_in, total, fx,
    ds_part, ds_cx, ds_out, ds_in,
    load, ag_send, ag_recv, x_send, gx_send, gx_recv, cx_send, cx_recv, rs_send, rs_recv, fx_send, fx_recv,
    dsc_send, dsc_recv, ds_send, ds_recv,
):
    n_z = n_doc // 2
    chips = n_layer // 2
    n_y = chips // 2
    docs, keep = g_own.shape
    shared = keep - swap
    rows = q_own.shape[0]
    sub = rows // 4
    piece = docs // PIECES
    doc = lax.axis_index("doc")
    layer = lax.axis_index("layer")
    col = doc // n_z
    z = lax.rem(doc, n_z)
    core = lax.rem(layer, 2)
    chip = layer // 2
    x_hi = chip // n_y
    y = lax.rem(chip, n_y)

    def doc_at(c, dz):
        return c * n_z + lax.rem(z + (dz + n_z), n_z)

    def chip_dev(c):
        return (doc, 2 * c + core)

    up = (doc_at(col, 1), layer)
    down = (doc_at(col, -1), layer)
    across = (doc_at(1 - col, 0), layer)
    twin = (doc, 2 * chip + 1 - core)
    far = (doc_at(1 - col, 0), 2 * ((1 - x_hi) * n_y + y) + core)

    barrier = pltpu.get_barrier_semaphore()
    for dev in (up, down, across, twin, far):
        pl.semaphore_signal(barrier, inc=1, device_id=dev, device_id_type=MESH)

    def greet(k, carry):
        pl.semaphore_signal(barrier, inc=1, device_id=chip_dev(lax.rem(chip + k, chips)), device_id_type=MESH)
        return carry

    lax.fori_loop(1, chips, greet, 0)

    mine = pl.ds(pl.multiple_of(col * swap, 128), swap)
    theirs = pl.ds(pl.multiple_of((1 - col) * swap, 128), swap)
    common = pl.ds(2 * swap, shared)
    first, rest = pl.ds(0, swap), pl.ds(swap, shared)
    loads = [
        (q_hbm.at[:, mine], q_own.at[:, first]),
        (q_hbm.at[:, common], q_own.at[:, rest]),
        (q_hbm.at[:, theirs], q_oth),
        (pc_hbm.at[:, mine], pc_own.at[:, first]),
        (pc_hbm.at[:, common], pc_own.at[:, rest]),
        (pc_hbm.at[:, theirs], pc_oth),
    ]
    n_small = len(loads)
    for i in range(PIECES):
        r = pl.ds(i * piece, piece)
        loads.append((g_hbm.at[r, theirs], g_send.at[r]))
    loads.append((g_hbm.at[:, mine], g_own.at[:, first]))
    loads.append((g_hbm.at[:, common], g_own.at[:, rest]))
    loads = [pltpu.make_async_copy(src, dst, load.at[i]) for i, (src, dst) in enumerate(loads)]
    for copy in loads:
        copy.start()
    for copy in loads[:n_small]:
        copy.wait()
    pre_own = (q_own[...].astype(F32) * pc_own[...]).astype(BF16)
    pre_oth = (q_oth[...].astype(F32) * pc_oth[...]).astype(BF16)
    for p in range(2):
        for k in range(2):
            r = slice((2 * k + p) * sub, (2 * k + p + 1) * sub)
            gath[p, 0, 0, k] = pre_own[r]
            px[p, k, :, :swap] = pre_oth[r]
            px[p, k, :, swap:] = pre_own[r, swap:]
    pl.semaphore_wait(barrier, 5 + chips - 1)

    def wait_for(ref, sem):
        pltpu.make_async_copy(ref, ref, sem).wait()

    seen = set()
    whole = set()

    def block(p, place, o, k=None):
        return gath.at[p, place, o] if k is None else gath.at[p, place, o, k]

    def send(p, src, dst, o, k, dev):
        pltpu.make_async_remote_copy(
            src_ref=block(p, src, o, k), dst_ref=block(p, dst, o, k),
            send_sem=ag_send, recv_sem=ag_recv.at[p, dst, o, k or 0], device_id=dev, device_id_type=MESH,
        ).start()

    def arrived(p, place, o, k):
        k = None if (p, place, o) in whole else k
        if (p, place, o, k) not in seen and (place, o) != (0, 0):
            seen.add((p, place, o, k))
            wait_for(block(p, place, o, k), ag_recv.at[p, place, o, k or 0])

    def pass_on(o, hops, p, split=False):
        for dev, way, first in ((up, UP, 0), (down, DOWN, 1)):
            here = way[hops - 1] if hops else 0
            if hops == 3 or split:
                for k in (first, 1 - first) if hops < 3 else (first,):
                    arrived(p, here, o, k)
                    send(p, here, way[hops], o, k, dev)
            else:
                for k in range(2):
                    arrived(p, here, o, k)
                whole.add((p, way[hops], o))
                send(p, here, way[hops], o, None, dev)

    pass_on(0, 0, 0)
    for p in range(2):
        whole.add((p, 0, 1))
        pltpu.make_async_remote_copy(
            src_ref=px.at[p], dst_ref=gath.at[p, 0, 1],
            send_sem=x_send, recv_sem=ag_recv.at[p, 0, 1, 0], device_id=across, device_id_type=MESH,
        ).start()
    pass_on(0, 0, 1)
    for i in range(PIECES):
        loads[n_small + i].wait()
        r = pl.ds(i * piece, piece)
        pltpu.make_async_remote_copy(
            src_ref=g_send.at[r], dst_ref=g_oth.at[r],
            send_sem=gx_send, recv_sem=gx_recv.at[i], device_id=across, device_id_type=MESH,
        ).start()
    for copy in loads[n_small + PIECES :]:
        copy.wait()

    q_at = docs
    x_at = docs + EXTRA
    stages = []

    def exchange(region, c0, c1):
        n = len(stages)
        p, d0, d1, o0, o1 = region
        window, places, sides = pl.ds(c0, c1 - c0), pl.ds(d0, d1 - d0), pl.ds(o0, o1 - o0)
        pltpu.make_async_remote_copy(
            src_ref=part.at[1 - core, p, places, sides, :, window], dst_ref=cx.at[p, places, sides, :, window],
            send_sem=cx_send, recv_sem=cx_recv.at[n], device_id=twin, device_id_type=MESH,
        ).start()
        stages.append((region, c0, c1))

    def multiply(regions, own, x0, x1):
        blocks = []
        for p, d0, d1, o0, o1 in regions:
            for d in range(d0, d1):
                for o in range(o0, o1):
                    for k in range(2):
                        arrived(p, d, o, k)
            blocks.append(gath[p, d0:d1, o0:o1].reshape(-1, keep))
        flat = blocks[0] if len(blocks) == 1 else jnp.concatenate(blocks, axis=0)

        def store(value, c0, c1):
            at = 0
            for p, d0, d1, o0, o1 in regions:
                shape = (d1 - d0, o1 - o0, 2, sub, c1 - c0)
                size = math.prod(shape[:4])
                v = value[at : at + size].reshape(shape)
                at += size
                for k in range(2):
                    part[k, p, d0:d1, o0:o1, :, c0:c1] = v[:, :, k]

        if own:
            store(lax.dot_general(flat, g_own[...], NT, preferred_element_type=F32), 0, docs)
        if x1 > x0:
            weights = g_oth[x0 * piece : x1 * piece]
            dots = lax.dot_general(flat[:, :swap], weights, NT, preferred_element_type=F32)
            store(dots, x_at + x0 * piece, x_at + x1 * piece)
        if own:
            for p, d0, d1, o0, o1 in regions:
                for d in range(d0, d1):
                    for o in range(o0, o1):
                        for k in range(2):
                            v = gath[p, d, o, k].astype(F32)
                            if o == 1:
                                v = v[:, :swap]
                            sq = jnp.sum(v * v, axis=1, keepdims=True)
                            part[k, p, d, o, :, q_at:x_at] = jnp.broadcast_to(sq, (sub, EXTRA))
        fresh[0] = len(stages)
        for region in regions:
            exchange(region, 0 if own else x_at + x0 * piece, x_at + x1 * piece)

    done, fresh = [0], [0]

    def reduce_out(last=False):
        while done[0] < (len(stages) if last else fresh[0]):
            n = done[0]
            done[0] += 1
            (p, d0, d1, o0, o1), c0, c1 = stages[n]
            window, places, sides = pl.ds(c0, c1 - c0), pl.ds(d0, d1 - d0), pl.ds(o0, o1 - o0)
            wait_for(cx.at[p, places, sides, :, window], cx_recv.at[n])
            parts = ((o0, o1),) if p == 0 or o1 - o0 == 1 else ((0, 1), (1, 2))
            for d, (s0, s1) in [(d, side) for d in range(d0, d1) for side in parts]:
                u0, u1 = 2 * p + s0, 2 * p + s1
                units = pl.ds(u0, u1 - u0)
                late = 1 if u1 == 4 else 0
                v = part[core, p, d, s0:s1, :, c0:c1] + cx[p, d, s0:s1, :, c0:c1]
                if c0 <= q_at < c1:
                    sq = v[..., q_at - c0 : x_at - c0]
                    high = sq.astype(BF16).astype(F32)
                    low = (sq - high).astype(BF16).astype(F32)
                    lane = lax.broadcasted_iota(jnp.int32, sq.shape, 2)
                    rs_out[d, u0:u1, :, q_at:x_at] = jnp.where(lane < EXTRA // 2, high, low).astype(BF16)
                    rs_out[d, u0:u1, :, c0:q_at] = v[..., : q_at - c0].astype(BF16)
                    if c1 > x_at:
                        rs_out[d, u0:u1, :, x_at:c1] = v[..., x_at - c0 :].astype(BF16)
                else:
                    rs_out[d, u0:u1, :, c0:c1] = v.astype(BF16)
                owner = lax.rem(z + (OFFSETS[d] + n_z), n_z)

                @pl.when(owner != y)
                def _(d=d, units=units, late=late):
                    pltpu.make_async_remote_copy(
                        src_ref=rs_out.at[d, units, :, window], dst_ref=rs_in.at[y, units, :, window],
                        send_sem=rs_send, recv_sem=rs_recv.at[late],
                        device_id=chip_dev(x_hi * n_y + owner), device_id_type=MESH,
                    ).start()

                @pl.when(owner == y)
                def _(d=d, u0=u0, u1=u1):
                    rs_in[y, u0:u1, :, c0:c1] = rs_out[d, u0:u1, :, c0:c1]

    def doc_squares():
        step = 64
        sums = []
        for i in range(docs // step):
            r = slice(i * step, (i + 1) * step)
            acc = jnp.zeros((step, 128), F32)
            for ref in (g_own, g_send):
                for k in range(ref.shape[1] // 128):
                    v = ref[r, k * 128 : (k + 1) * 128].astype(F32)
                    acc = acc + v * v
            sums.append(acc)
        lanes = jnp.concatenate(sums, axis=0)
        ones = jnp.ones((8, 128), F32)
        sq = lax.dot_general(ones, lanes, NT, preferred_element_type=F32, precision=lax.Precision.HIGHEST)
        ds_part[...] = sq[0:1]
        pltpu.make_async_remote_copy(
            src_ref=ds_part, dst_ref=ds_cx, send_sem=dsc_send, recv_sem=dsc_recv, device_id=twin, device_id_type=MESH
        ).start()

    def doc_spread():
        wait_for(ds_cx, dsc_recv)
        ds_out[...] = ds_part[...] + ds_cx[...]
        ds_in[chip] = ds_out[...]

        def spread(k, carry):
            pltpu.make_async_remote_copy(
                src_ref=ds_out, dst_ref=ds_in.at[chip], send_sem=ds_send, recv_sem=ds_recv,
                device_id=chip_dev(lax.rem(chip + k, chips)), device_id_type=MESH,
            ).start()
            return carry

        lax.fori_loop(1, chips, spread, 0)

    def piece_here(i):
        r = pl.ds(i * piece, piece)
        wait_for(g_oth.at[r], gx_recv.at[i])

    def sum_along_y(o, p):
        acc = rs_in[0, 2 * p + o].astype(F32)
        for k in range(1, n_y):
            acc = acc + rs_in[k, 2 * p + o].astype(F32)
        total[o, p * sub : (p + 1) * sub] = acc

    span = docs + EXTRA

    def send_along_x(o, r0, r1):
        r = pl.ds(r0, r1 - r0)
        owner_hi = lax.rem(col + o, 2)
        other = lax.rem(owner_hi + x_hi, 2)
        row_dev = 2 * (owner_hi * n_y + y) + core
        pltpu.make_async_remote_copy(
            src_ref=total.at[o, r, pl.ds(q_at, span)], dst_ref=fx.at[2 * other, r],
            send_sem=fx_send, recv_sem=fx_recv.at[2 * other],
            device_id=(doc_at(1 - col, 0), row_dev), device_id_type=MESH,
        ).start()

        @pl.when(owner_hi != x_hi)
        def _():
            pltpu.make_async_remote_copy(
                src_ref=total.at[o, r, pl.ds(0, span)], dst_ref=fx.at[1, r],
                send_sem=fx_send, recv_sem=fx_recv.at[1],
                device_id=(doc, row_dev), device_id_type=MESH,
            ).start()

    doc_squares()
    pass_on(1, 0, 0)
    pass_on(0, 1, 0)
    pass_on(0, 1, 1)
    multiply([(0, 0, 1, 0, 2), (0, 1, 3, 0, 1), (1, 0, 1, 0, 2), (1, 1, 3, 0, 1)], True, 0, 0)
    doc_spread()
    pass_on(1, 1, 0)
    reduce_out(last=True)
    pass_on(0, 2, 0)
    pass_on(1, 0, 1)
    multiply([(0, 1, 3, 1, 2), (0, 3, 5, 0, 2)], True, 0, 0)
    piece_here(0)
    multiply([(0, 0, 5, 0, 2), (1, 0, 1, 0, 2), (1, 1, 3, 0, 1)], False, 0, 1)
    reduce_out()
    pass_on(0, 2, 1)
    pass_on(1, 2, 0)
    reduce_out(last=True)
    pass_on(0, 3, 0)
    multiply([(1, 3, 5, 0, 1), (0, 5, 7, 0, 1)], True, 0, 1)
    piece_here(1)
    multiply([(0, 0, 5, 0, 2), (0, 5, 7, 0, 1), (1, 0, 1, 0, 2), (1, 1, 5, 0, 1)], False, 1, 2)
    reduce_out()
    pass_on(1, 1, 1)
    reduce_out(last=True)
    pass_on(0, 3, 1)
    multiply([(1, 1, 3, 1, 2), (1, 5, 7, 0, 1)], True, 0, 2)
    pass_on(1, 3, 0)
    reduce_out(last=True)
    multiply([(0, 5, 7, 1, 2), (0, 7, 8, 0, 1)], True, 0, 2)
    piece_here(2)
    multiply([(0, 0, 7, 0, 2), (0, 7, 8, 0, 1), (1, 0, 3, 0, 2), (1, 3, 7, 0, 1)], False, 2, 3)
    reduce_out()
    pass_on(1, 2, 1, split=True)
    reduce_out(last=True)
    multiply([(1, 3, 5, 1, 2), (1, 7, 8, 0, 1), (0, 7, 8, 1, 2)], True, 0, 3)
    piece_here(3)
    multiply([(0, 0, 8, 0, 2), (1, 0, 5, 0, 2), (1, 5, 8, 0, 1)], False, 3, 4)
    pass_on(1, 3, 1)
    reduce_out()
    multiply([(1, 5, 7, 1, 2)], True, 0, 4)
    reduce_out()
    multiply([(1, 7, 8, 1, 2)], True, 0, 4)
    reduce_out(last=True)

    wait_for(rs_in.at[pl.ds(0, n_y - 1), pl.ds(0, 3)], rs_recv.at[0])
    sum_along_y(0, 0)
    sum_along_y(0, 1)
    sum_along_y(1, 0)
    send_along_x(0, 0, 2 * sub)
    send_along_x(1, 0, sub)
    wait_for(ds_in.at[pl.ds(0, chips - 1)], ds_recv)
    doc_total = jnp.sum(ds_in[...], axis=0)
    wait_for(rs_in.at[pl.ds(0, n_y - 1), 3], rs_recv.at[1])
    sum_along_y(1, 1)
    send_along_x(1, sub, 2 * sub)
    here = total[lax.rem(x_hi + col, 2), :, 0:span]
    for i in range(3):
        wait_for(fx.at[i], fx_recv.at[i])
    dots = here[:, :docs] + fx[1, :, :docs] + fx[0, :, EXTRA:] + fx[2, :, EXTRA:]
    sq = here[:, docs:] + fx[1, :, docs:] + fx[0, :, :EXTRA] + fx[2, :, :EXTRA]
    query_sq = sq[:, 0:1] + sq[:, EXTRA // 2 : EXTRA // 2 + 1]
    out_ref[...] = factor * dots * lax.rsqrt(query_sq + 1e-06) * lax.rsqrt(doc_total + 1e-06)

    wait_for(gath.at[:, pl.ds(0, 7)], ag_send)
    wait_for(px, x_send)
    wait_for(g_oth, gx_send)
    wait_for(cx, cx_send)
    wait_for(rs_out.at[pl.ds(0, n_y - 1)], rs_send)
    wait_for(fx, fx_send)
    wait_for(ds_cx, dsc_send)
    wait_for(ds_in.at[pl.ds(0, chips - 1)], ds_send)


def shards(grads, queries, precond):
    n_doc = lax.axis_size("doc")
    n_layer = lax.axis_size("layer")
    docs, width = grads.shape[0], grads.shape[2]
    rows = queries.shape[0]
    chips = n_layer // 2
    n_y = chips // 2
    own_rows = rows * n_doc // n_layer
    swap = width * 7 // 16
    keep = width - swap
    sub = rows // 4
    places = len(OFFSETS)
    wide = 2 * docs + EXTRA
    factor = math.sqrt(n_layer * width)
    dma = pltpu.SemaphoreType.DMA
    return pl.pallas_call(
        functools.partial(kernel, n_doc, n_layer, swap, factor),
        out_shape=jax.ShapeDtypeStruct((own_rows, docs), F32),
        in_specs=[pl.BlockSpec(memory_space=pltpu.HBM)] * 3,
        out_specs=pl.BlockSpec(memory_space=pltpu.VMEM),
        scratch_shapes=[
            pltpu.VMEM((docs, keep), BF16),
            pltpu.VMEM((docs, swap), BF16),
            pltpu.VMEM((docs, swap), BF16),
            pltpu.VMEM((rows, keep), BF16),
            pltpu.VMEM((rows, swap), BF16),
            pltpu.VMEM((1, keep), F32),
            pltpu.VMEM((1, swap), F32),
            pltpu.VMEM((2, places, 2, 2, sub, keep), BF16),
            pltpu.VMEM((2, 2, sub, keep), BF16),
            pltpu.VMEM((2, 2, places, 2, sub, wide), F32),
            pltpu.VMEM((2, places, 2, sub, wide), F32),
            pltpu.VMEM((places, 4, sub, wide), BF16),
            pltpu.VMEM((n_y, 4, sub, wide), BF16),
            pltpu.VMEM((2, 2 * sub, wide), F32),
            pltpu.VMEM((3, 2 * sub, docs + EXTRA), F32),
            pltpu.VMEM((1, docs), F32),
            pltpu.VMEM((1, docs), F32),
            pltpu.VMEM((1, docs), F32),
            pltpu.VMEM((chips, 1, docs), F32),
            dma((8 + PIECES,)), dma, dma((2, places, 2, 2)), dma, dma, dma((PIECES,)), dma, dma((64,)),
            dma, dma((2,)), dma, dma((3,)), dma, dma, dma, dma,
        ],
        compiler_params=pltpu.CompilerParams(
            collective_id=0, has_side_effects=True, vmem_limit_bytes=48 << 20
        ),
        cost_estimate=pl.CostEstimate(
            flops=2 * rows * n_doc * docs * width, bytes_accessed=2 * docs * width, transcendentals=0
        ),
        name="gather_multiply_reduce",
    )(grads.reshape(docs, width), queries.reshape(rows, width), precond)


def solution(mesh):
    placed = (P("doc", "layer", None), P("doc", "layer", None), P("layer", None))
    return jax.shard_map(
        shards, mesh=mesh, in_specs=placed, out_specs=P("layer", "doc"), check_vma=False
    )
```

time: 435 us -> 85.5 us (0.20)
  blocking collectives: 179 us -> 0 us
  waiting for transfers between devices: 143 us -> 0 us
  Pallas kernels: 0 us -> 79.5 us
  matrix products: 57.3 us -> 0 us
  starting transfers between devices: 31.7 us -> 0 us
  between operations: 13.4 us -> 0.01 us
  other arithmetic: 6.04 us -> 0 us
    psum x2 -> x0, blocking collectives: 179 us -> none  [the longest x1 114 us: shards(): query_total = lax.psum(placed, ('doc', 'layer'))]
    ppermute x15 -> x0, waiting for transfers between devices: 143 us -> none  [passed_along(): return lax.ppermute(block, axis, route)]
    pallas_call x0 -> x1, Pallas kernels: none -> 79.5 us  [shards(): pl.pallas_call(functools.partial(kernel, n_doc, n_layer, swap, factor), o...]
    dot_general x16 -> x0, matrix products: 57.3 us -> none  [visit(): lax.dot_general(piece, flat_grads, (((1,), (1,)), ((), ())), preferred_el...]
    ppermute x15 -> x0, starting transfers between devices: 31.7 us -> none  [passed_along(): return lax.ppermute(block, axis, route)]
    reduce_sum x2 -> x0, other arithmetic: 4.41 us -> none  [the longest x1 3.1 us: shards(): doc_sq = jnp.sum(jnp.square(flat_grads.astype(jnp.float32)), axis=1)]
  transfers between devices with their start and end apart: 16 -> 0, of which waited for: 15 -> 0; matrix products, arithmetic and copies ran while one was open for 13% -> 0% of each run, Pallas kernels for 0% -> 0%
where the time goes in v2:
time: 85.5 us; the launch traced here: 84.1 us
  Pallas kernels  79.5 us (93%)
  local copies, waits for them, and re-layouts  4.58 us (5%)
    pallas_call x1, Pallas kernels, shards(): pl.pallas_call(functools.partial(kernel, n_doc, n_layer, swap, factor), o...  79.5 us
    unnamed x7, local copies, waits for them, and re-layouts  4.58 us

profile of v2, /device:TPU:1, one launch (start us, length us, event | category | flops | bytes accessed | tf_op | source)
XLA Modules:
  0.0 84.1 jit_solution(15808258911310945213)
XLA Ops:
  0.0 0.0 copy-start
  0.0 2.2 %copy-done = bf16[512,1,4096]{2,0,1:T(8,128)(2,1)S(1)} copy-done((bf16[512,1,4096]{2,0,1:T(8,128)(2,1)S(1)}, bf16[512,1,4096]{2,0,1:T(8,128)(2,1)}, u32[]{:S(2)}) %copy-start) | copy-done | bytes 4194328
  2.2 0.0 copy-start.1
  2.2 1.0 %copy-done.1 = bf16[64,1,4096]{2,0,1:T(8,128)(2,1)S(1)} copy-done((bf16[64,1,4096]{2,0,1:T(8,128)(2,1)S(1)}, bf16[64,1,4096]{2,0,1:T(8,128)(2,1)}, u32[]{:S(2)}) %copy-start.1) | copy-done | bytes 524312
  3.2 0.0 copy-start.2
  3.2 0.7 copy-done.2
  3.9 79.5 %gather_multiply_reduce.1 = f32[32,512]{1,0:T(8,128)S(1)} custom-call(bf16[512,4096]{1,0:T(8,128)(2,1)S(1)} %bitcast.2, bf16[64,4096]{1,0:T(8,128)(2,1)S(1)} %bitcast.3, f32[1,4096]{1,0:T(1,128)S(1)} %copy-done.2), custom_call_target="tpu_custom_call" | custom-call | flops 4294967296 | bytes 4194304 | tf_op jit(solution)/shard_map/gather_multiply_reduce/pallas_call | solution.py:401
  83.5 0.6 copy.5
Async XLA Ops:
  0.0 2.2 %copy-start = (bf16[512,1,4096]{2,0,1:T(8,128)(2,1)S(1)}, bf16[512,1,4096]{2,0,1:T(8,128)(2,1)}, u32[]{:S(2)}) copy-start(bf16[512,1,4096]{2,0,1:T(8,128)(2,1)} %param.3) | copy-start | bytes 12582916
  2.2 1.0 %copy-start.1 = (bf16[64,1,4096]{2,0,1:T(8,128)(2,1)S(1)}, bf16[64,1,4096]{2,0,1:T(8,128)(2,1)}, u32[]{:S(2)}) copy-start(bf16[64,1,4096]{2,0,1:T(8,128)(2,1)} %param.4) | copy-start | bytes 1572868
  3.2 0.7 copy-start.2

commit v3 on v2

--- a/solution.py
+++ b/solution.py
@@ -23,7 +23,7 @@
 def kernel(
     n_doc, n_layer, swap, factor,
     g_hbm, q_hbm, pc_hbm, out_ref,
-    g_own, g_send, g_oth, q_own, q_oth, pc_own, pc_oth, gath, px, part, cx, rs_out, rs_in, total, fx,
+    g_own, g_send, g_oth, q_own, q_oth, pc_own, pc_oth, gath, px, part, cx, rs_out, rs_in, total, fx_out, fx,
     ds_part, ds_cx, ds_out, ds_in,
     load, ag_send, ag_recv, x_send, gx_send, gx_recv, cx_send, cx_recv, rs_send, rs_recv, fx_send, fx_recv,
     dsc_send, dsc_recv, ds_send, ds_recv,
@@ -57,16 +57,6 @@
     twin = (doc, 2 * chip + 1 - core)
     far = (doc_at(1 - col, 0), 2 * ((1 - x_hi) * n_y + y) + core)
 
-    barrier = pltpu.get_barrier_semaphore()
-    for dev in (up, down, across, twin, far):
-        pl.semaphore_signal(barrier, inc=1, device_id=dev, device_id_type=MESH)
-
-    def greet(k, carry):
-        pl.semaphore_signal(barrier, inc=1, device_id=chip_dev(lax.rem(chip + k, chips)), device_id_type=MESH)
-        return carry
-
-    lax.fori_loop(1, chips, greet, 0)
-
     mine = pl.ds(pl.multiple_of(col * swap, 128), swap)
     theirs = pl.ds(pl.multiple_of((1 - col) * swap, 128), swap)
     common = pl.ds(2 * swap, shared)
@@ -86,7 +76,20 @@
     loads.append((g_hbm.at[:, mine], g_own.at[:, first]))
     loads.append((g_hbm.at[:, common], g_own.at[:, rest]))
     loads = [pltpu.make_async_copy(src, dst, load.at[i]) for i, (src, dst) in enumerate(loads)]
-    for copy in loads:
+    for copy in loads[:n_small]:
+        copy.start()
+
+    barrier = pltpu.get_barrier_semaphore()
+    for dev in (up, down, across, twin, far):
+        pl.semaphore_signal(barrier, inc=1, device_id=dev, device_id_type=MESH)
+
+    def greet(k, carry):
+        pl.semaphore_signal(barrier, inc=1, device_id=chip_dev(lax.rem(chip + k, chips)), device_id_type=MESH)
+        return carry
+
+    lax.fori_loop(1, chips, greet, 0)
+
+    for copy in loads[n_small:]:
         copy.start()
     for copy in loads[:n_small]:
         copy.wait()
@@ -154,17 +157,19 @@
 
     q_at = docs
     x_at = docs + EXTRA
-    stages = []
+    batches = []
+    count = [0]
 
     def exchange(region, c0, c1):
-        n = len(stages)
+        n = count[0]
+        count[0] += 1
         p, d0, d1, o0, o1 = region
         window, places, sides = pl.ds(c0, c1 - c0), pl.ds(d0, d1 - d0), pl.ds(o0, o1 - o0)
         pltpu.make_async_remote_copy(
             src_ref=part.at[1 - core, p, places, sides, :, window], dst_ref=cx.at[p, places, sides, :, window],
             send_sem=cx_send, recv_sem=cx_recv.at[n], device_id=twin, device_id_type=MESH,
         ).start()
-        stages.append((region, c0, c1))
+        batches[-1].append((n, region, c0, c1))
 
     def multiply(regions, own, x0, x1):
         blocks = []
@@ -202,49 +207,63 @@
                                 v = v[:, :swap]
                             sq = jnp.sum(v * v, axis=1, keepdims=True)
                             part[k, p, d, o, :, q_at:x_at] = jnp.broadcast_to(sq, (sub, EXTRA))
-        fresh[0] = len(stages)
+        batches.append([])
         for region in regions:
             exchange(region, 0 if own else x_at + x0 * piece, x_at + x1 * piece)
 
-    done, fresh = [0], [0]
-
-    def reduce_out(last=False):
-        while done[0] < (len(stages) if last else fresh[0]):
-            n = done[0]
-            done[0] += 1
-            (p, d0, d1, o0, o1), c0, c1 = stages[n]
+    done = [0]
+
+    def high_low(sq):
+        high = sq.astype(BF16).astype(F32)
+        low = (sq - high).astype(BF16).astype(F32)
+        lane = lax.broadcasted_iota(jnp.int32, sq.shape, sq.ndim - 1)
+        return jnp.where(lane < EXTRA // 2, high, low).astype(BF16)
+
+    def reduce_batch(batch):
+        units_of = {}
+        for n, (p, d0, d1, o0, o1), c0, c1 in batch:
             window, places, sides = pl.ds(c0, c1 - c0), pl.ds(d0, d1 - d0), pl.ds(o0, o1 - o0)
             wait_for(cx.at[p, places, sides, :, window], cx_recv.at[n])
-            parts = ((o0, o1),) if p == 0 or o1 - o0 == 1 else ((0, 1), (1, 2))
-            for d, (s0, s1) in [(d, side) for d in range(d0, d1) for side in parts]:
-                u0, u1 = 2 * p + s0, 2 * p + s1
-                units = pl.ds(u0, u1 - u0)
-                late = 1 if u1 == 4 else 0
-                v = part[core, p, d, s0:s1, :, c0:c1] + cx[p, d, s0:s1, :, c0:c1]
-                if c0 <= q_at < c1:
-                    sq = v[..., q_at - c0 : x_at - c0]
-                    high = sq.astype(BF16).astype(F32)
-                    low = (sq - high).astype(BF16).astype(F32)
-                    lane = lax.broadcasted_iota(jnp.int32, sq.shape, 2)
-                    rs_out[d, u0:u1, :, q_at:x_at] = jnp.where(lane < EXTRA // 2, high, low).astype(BF16)
-                    rs_out[d, u0:u1, :, c0:q_at] = v[..., : q_at - c0].astype(BF16)
-                    if c1 > x_at:
-                        rs_out[d, u0:u1, :, x_at:c1] = v[..., x_at - c0 :].astype(BF16)
+            u0, u1 = 2 * p + o0, 2 * p + o1
+            v = part[core, p, d0:d1, o0:o1, :, c0:c1] + cx[p, d0:d1, o0:o1, :, c0:c1]
+            if c0 == 0:
+                rs_out[d0:d1, u0:u1, :, 0:q_at] = v[..., :q_at].astype(BF16)
+                rs_out[d0:d1, u0:u1, :, q_at:x_at] = high_low(v[..., q_at:x_at])
+                if c1 > x_at:
+                    rs_out[d0:d1, u0:u1, :, x_at:c1] = v[..., x_at:].astype(BF16)
+            else:
+                rs_out[d0:d1, u0:u1, :, c0:c1] = v.astype(BF16)
+            for d in range(d0, d1):
+                units_of.setdefault(d, []).append((u0, u1))
+        window = pl.ds(c0, c1 - c0)
+        for d in sorted(units_of, key=lambda d: -d):
+            runs = []
+            for u0, u1 in sorted(units_of[d]):
+                if runs and runs[-1][1] == u0:
+                    runs[-1] = (runs[-1][0], u1)
                 else:
-                    rs_out[d, u0:u1, :, c0:c1] = v.astype(BF16)
-                owner = lax.rem(z + (OFFSETS[d] + n_z), n_z)
-
-                @pl.when(owner != y)
-                def _(d=d, units=units, late=late):
+                    runs.append((u0, u1))
+            owner = lax.rem(z + (OFFSETS[d] + n_z), n_z)
+
+            @pl.when(owner != y)
+            def _(d=d, runs=runs, owner=owner):
+                for u0, u1 in runs:
+                    units = pl.ds(u0, u1 - u0)
                     pltpu.make_async_remote_copy(
                         src_ref=rs_out.at[d, units, :, window], dst_ref=rs_in.at[y, units, :, window],
-                        send_sem=rs_send, recv_sem=rs_recv.at[late],
+                        send_sem=rs_send, recv_sem=rs_recv,
                         device_id=chip_dev(x_hi * n_y + owner), device_id_type=MESH,
                     ).start()
 
-                @pl.when(owner == y)
-                def _(d=d, u0=u0, u1=u1):
+            @pl.when(owner == y)
+            def _(d=d, runs=runs):
+                for u0, u1 in runs:
                     rs_in[y, u0:u1, :, c0:c1] = rs_out[d, u0:u1, :, c0:c1]
+
+    def reduce_out(last=False):
+        while done[0] < len(batches) - (0 if last else 1):
+            reduce_batch(batches[done[0]])
+            done[0] += 1
 
     def doc_squares():
         step = 64
@@ -291,13 +310,17 @@
 
     span = docs + EXTRA
 
-    def send_along_x(o, r0, r1):
-        r = pl.ds(r0, r1 - r0)
+    def send_along_x(o):
+        v = total[o]
+        sq = v[:, q_at : q_at + 1] + v[:, q_at + EXTRA // 2 : q_at + EXTRA // 2 + 1]
+        fx_out[o, :, 0:q_at] = v[:, 0:q_at].astype(BF16)
+        fx_out[o, :, q_at:x_at] = high_low(jnp.broadcast_to(sq, (2 * sub, EXTRA)))
+        fx_out[o, :, x_at:] = v[:, x_at:].astype(BF16)
         owner_hi = lax.rem(col + o, 2)
         other = lax.rem(owner_hi + x_hi, 2)
         row_dev = 2 * (owner_hi * n_y + y) + core
         pltpu.make_async_remote_copy(
-            src_ref=total.at[o, r, pl.ds(q_at, span)], dst_ref=fx.at[2 * other, r],
+            src_ref=fx_out.at[o, :, pl.ds(q_at, span)], dst_ref=fx.at[2 * other],
             send_sem=fx_send, recv_sem=fx_recv.at[2 * other],
             device_id=(doc_at(1 - col, 0), row_dev), device_id_type=MESH,
         ).start()
@@ -305,71 +328,69 @@
         @pl.when(owner_hi != x_hi)
         def _():
             pltpu.make_async_remote_copy(
-                src_ref=total.at[o, r, pl.ds(0, span)], dst_ref=fx.at[1, r],
+                src_ref=fx_out.at[o, :, pl.ds(0, span)], dst_ref=fx.at[1],
                 send_sem=fx_send, recv_sem=fx_recv.at[1],
                 device_id=(doc, row_dev), device_id_type=MESH,
             ).start()
 
     doc_squares()
+    pass_on(0, 1, 0)
     pass_on(1, 0, 0)
-    pass_on(0, 1, 0)
-    pass_on(0, 1, 1)
     multiply([(0, 0, 1, 0, 2), (0, 1, 3, 0, 1), (1, 0, 1, 0, 2), (1, 1, 3, 0, 1)], True, 0, 0)
     doc_spread()
+    pass_on(0, 2, 0)
+    reduce_out(last=True)
     pass_on(1, 1, 0)
-    reduce_out(last=True)
-    pass_on(0, 2, 0)
+    multiply([(0, 3, 5, 0, 1), (0, 1, 3, 1, 2)], True, 0, 0)
+    piece_here(0)
+    multiply([(0, 0, 3, 0, 2), (0, 3, 5, 0, 1), (1, 0, 1, 0, 2), (1, 1, 3, 0, 1)], False, 0, 1)
+    pass_on(0, 3, 0)
+    reduce_out()
+    pass_on(1, 2, 0)
+    pass_on(0, 1, 1)
+    reduce_out(last=True)
+    multiply([(0, 5, 8, 0, 1), (0, 3, 5, 1, 2)], True, 0, 1)
+    piece_here(1)
+    multiply([(0, 0, 5, 0, 2), (0, 5, 8, 0, 1), (1, 0, 1, 0, 2), (1, 1, 3, 0, 1)], False, 1, 2)
+    pass_on(1, 3, 0)
     pass_on(1, 0, 1)
-    multiply([(0, 1, 3, 1, 2), (0, 3, 5, 0, 2)], True, 0, 0)
-    piece_here(0)
-    multiply([(0, 0, 5, 0, 2), (1, 0, 1, 0, 2), (1, 1, 3, 0, 1)], False, 0, 1)
     reduce_out()
     pass_on(0, 2, 1)
-    pass_on(1, 2, 0)
-    reduce_out(last=True)
-    pass_on(0, 3, 0)
-    multiply([(1, 3, 5, 0, 1), (0, 5, 7, 0, 1)], True, 0, 1)
-    piece_here(1)
-    multiply([(0, 0, 5, 0, 2), (0, 5, 7, 0, 1), (1, 0, 1, 0, 2), (1, 1, 5, 0, 1)], False, 1, 2)
+    reduce_out(last=True)
+    multiply([(0, 5, 8, 1, 2), (1, 3, 5, 0, 1)], True, 0, 2)
+    pass_on(1, 1, 1)
+    reduce_out(last=True)
+    piece_here(2)
+    multiply([(0, 0, 8, 0, 2), (1, 0, 1, 0, 2), (1, 1, 5, 0, 1)], False, 2, 3)
+    pass_on(0, 3, 1)
     reduce_out()
-    pass_on(1, 1, 1)
-    reduce_out(last=True)
-    pass_on(0, 3, 1)
-    multiply([(1, 1, 3, 1, 2), (1, 5, 7, 0, 1)], True, 0, 2)
-    pass_on(1, 3, 0)
-    reduce_out(last=True)
-    multiply([(0, 5, 7, 1, 2), (0, 7, 8, 0, 1)], True, 0, 2)
-    piece_here(2)
-    multiply([(0, 0, 7, 0, 2), (0, 7, 8, 0, 1), (1, 0, 3, 0, 2), (1, 3, 7, 0, 1)], False, 2, 3)
+    multiply([(1, 1, 3, 1, 2), (1, 5, 7, 0, 1)], True, 0, 3)
+    pass_on(1, 2, 1, split=True)
+    reduce_out(last=True)
+    multiply([(1, 3, 5, 1, 2), (1, 7, 8, 0, 1)], True, 0, 3)
     reduce_out()
-    pass_on(1, 2, 1, split=True)
-    reduce_out(last=True)
-    multiply([(1, 3, 5, 1, 2), (1, 7, 8, 0, 1), (0, 7, 8, 1, 2)], True, 0, 3)
+    pass_on(1, 3, 1)
     piece_here(3)
     multiply([(0, 0, 8, 0, 2), (1, 0, 5, 0, 2), (1, 5, 8, 0, 1)], False, 3, 4)
-    pass_on(1, 3, 1)
-    reduce_out()
+    reduce_out(last=True)
     multiply([(1, 5, 7, 1, 2)], True, 0, 4)
-    reduce_out()
+    reduce_out(last=True)
     multiply([(1, 7, 8, 1, 2)], True, 0, 4)
     reduce_out(last=True)
 
-    wait_for(rs_in.at[pl.ds(0, n_y - 1), pl.ds(0, 3)], rs_recv.at[0])
-    sum_along_y(0, 0)
-    sum_along_y(0, 1)
-    sum_along_y(1, 0)
-    send_along_x(0, 0, 2 * sub)
-    send_along_x(1, 0, sub)
+    wait_for(rs_in.at[pl.ds(0, n_y - 1)], rs_recv)
+    for o in range(2):
+        for p in range(2):
+            sum_along_y(o, p)
+        send_along_x(o)
     wait_for(ds_in.at[pl.ds(0, chips - 1)], ds_recv)
     doc_total = jnp.sum(ds_in[...], axis=0)
-    wait_for(rs_in.at[pl.ds(0, n_y - 1), 3], rs_recv.at[1])
-    sum_along_y(1, 1)
-    send_along_x(1, sub, 2 * sub)
     here = total[lax.rem(x_hi + col, 2), :, 0:span]
     for i in range(3):
         wait_for(fx.at[i], fx_recv.at[i])
-    dots = here[:, :docs] + fx[1, :, :docs] + fx[0, :, EXTRA:] + fx[2, :, EXTRA:]
-    sq = here[:, docs:] + fx[1, :, docs:] + fx[0, :, :EXTRA] + fx[2, :, :EXTRA]
+    got = [fx[i].astype(F32) for i in range(3)]
+    dots = here[:, :docs] + got[1][:, :docs] + got[0][:, EXTRA:] + got[2][:, EXTRA:]
+    sq = here[:, docs:] + got[1][:, docs:] + got[0][:, :EXTRA] + got[2][:, :EXTRA]
     query_sq = sq[:, 0:1] + sq[:, EXTRA // 2 : EXTRA // 2 + 1]
     out_ref[...] = factor * dots * lax.rsqrt(query_sq + 1e-06) * lax.rsqrt(doc_total + 1e-06)
 
@@ -391,7 +412,7 @@
     chips = n_layer // 2
     n_y = chips // 2
     own_rows = rows * n_doc // n_layer
-    swap = width * 7 // 16
+    swap = width * 13 // 32
     keep = width - swap
     sub = rows // 4
     places = len(OFFSETS)
@@ -418,16 +439,17 @@
             pltpu.VMEM((places, 4, sub, wide), BF16),
             pltpu.VMEM((n_y, 4, sub, wide), BF16),
             pltpu.VMEM((2, 2 * sub, wide), F32),
-            pltpu.VMEM((3, 2 * sub, docs + EXTRA), F32),
+            pltpu.VMEM((2, 2 * sub, wide), BF16),
+            pltpu.VMEM((3, 2 * sub, docs + EXTRA), BF16),
             pltpu.VMEM((1, docs), F32),
             pltpu.VMEM((1, docs), F32),
             pltpu.VMEM((1, docs), F32),
             pltpu.VMEM((chips, 1, docs), F32),
             dma((8 + PIECES,)), dma, dma((2, places, 2, 2)), dma, dma, dma((PIECES,)), dma, dma((64,)),
-            dma, dma((2,)), dma, dma((3,)), dma, dma, dma, dma,
+            dma, dma, dma, dma((3,)), dma, dma, dma, dma,
         ],
         compiler_params=pltpu.CompilerParams(
-            collective_id=0, has_side_effects=True, vmem_limit_bytes=48 << 20
+            collective_id=0, has_side_effects=True, vmem_limit_bytes=63 << 20
         ),
         cost_estimate=pl.CostEstimate(
             flops=2 * rows * n_doc * docs * width, bytes_accessed=2 * docs * width, transcendentals=0

time: 85.5 us -> 82.2 us (0.961)
  the two profiles are of different devices: /device:TPU:1 before, /device:TPU:33 now
where the time goes in v3:
time: 82.2 us; the launch traced here: 82 us
  Pallas kernels  80.5 us (98%)
  local copies, waits for them, and re-layouts  1.47 us (2%)
    pallas_call x1, Pallas kernels, shards(): pl.pallas_call(functools.partial(kernel, n_doc, n_layer, swap, factor), o...  80.5 us

profile of v3, /device:TPU:33, one launch (start us, length us, event | category | flops | bytes accessed | tf_op | source)
XLA Modules:
  0.0 82.0 jit_solution(1642855244447904009)
XLA Ops:
  0.0 80.5 %gather_multiply_reduce.1 = f32[32,512]{1,0:T(8,128)} custom-call(bf16[512,4096]{1,0:T(8,128)(2,1)} %bitcast.2, bf16[64,4096]{1,0:T(8,128)(2,1)} %bitcast.3, f32[1,4096]{1,0:T(1,128)} %pc_hbm.1), custom_call_target="tpu_custom_call" | custom-call | flops 4294967296 | bytes 4194304 | tf_op jit(solution)/shard_map/gather_multiply_reduce/pallas_call | solution.py:422
  80.5 1.5 %copy.5 = f32[32,512]{1,0:T(8,128)} copy(f32[32,512]{1,0:T(8,128)} %gather_multiply_reduce.1) | data formatting | bytes 131072

commit v4 on v3

--- a/solution.py
+++ b/solution.py
@@ -16,6 +16,7 @@
 OFFSETS = (0, -1, 1, -2, 2, -3, 3, 4)
 UP = (1, 3, 5, 7)
 DOWN = (2, 4, 6, 7)
+FAR = ((1, 5, 7, 1, 2), (1, 7, 8, 1, 2))
 EXTRA = 128
 PIECES = 4
 
@@ -93,14 +94,16 @@
         copy.start()
     for copy in loads[:n_small]:
         copy.wait()
-    pre_own = (q_own[...].astype(F32) * pc_own[...]).astype(BF16)
-    pre_oth = (q_oth[...].astype(F32) * pc_oth[...]).astype(BF16)
-    for p in range(2):
+    shared_at = pl.ds(swap, shared)
+
+    def weigh(p):
         for k in range(2):
-            r = slice((2 * k + p) * sub, (2 * k + p + 1) * sub)
-            gath[p, 0, 0, k] = pre_own[r]
-            px[p, k, :, :swap] = pre_oth[r]
-            px[p, k, :, swap:] = pre_own[r, swap:]
+            r = pl.ds((2 * k + p) * sub, sub)
+            gath[p, 0, 0, k] = (q_own[r, :].astype(F32) * pc_own[...]).astype(BF16)
+            px[p, k, :, 0:swap] = (q_oth[r, :].astype(F32) * pc_oth[...]).astype(BF16)
+            px[p, k, :, shared_at] = gath[p, 0, 0, k, :, shared_at]
+
+    weigh(0)
     pl.semaphore_wait(barrier, 5 + chips - 1)
 
     def wait_for(ref, sem):
@@ -137,14 +140,15 @@
                 whole.add((p, way[hops], o))
                 send(p, here, way[hops], o, None, dev)
 
-    pass_on(0, 0, 0)
     for p in range(2):
+        if p == 1:
+            weigh(1)
+        pass_on(0, 0, p)
         whole.add((p, 0, 1))
         pltpu.make_async_remote_copy(
             src_ref=px.at[p], dst_ref=gath.at[p, 0, 1],
             send_sem=x_send, recv_sem=ag_recv.at[p, 0, 1, 0], device_id=across, device_id_type=MESH,
         ).start()
-    pass_on(0, 0, 1)
     for i in range(PIECES):
         loads[n_small + i].wait()
         r = pl.ds(i * piece, piece)
@@ -221,6 +225,7 @@
 
     def reduce_batch(batch):
         units_of = {}
+        late = 1 if batch[0][1] in FAR else 0
         for n, (p, d0, d1, o0, o1), c0, c1 in batch:
             window, places, sides = pl.ds(c0, c1 - c0), pl.ds(d0, d1 - d0), pl.ds(o0, o1 - o0)
             wait_for(cx.at[p, places, sides, :, window], cx_recv.at[n])
@@ -251,7 +256,7 @@
                     units = pl.ds(u0, u1 - u0)
                     pltpu.make_async_remote_copy(
                         src_ref=rs_out.at[d, units, :, window], dst_ref=rs_in.at[y, units, :, window],
-                        send_sem=rs_send, recv_sem=rs_recv,
+                        send_sem=rs_send, recv_sem=rs_recv.at[late],
                         device_id=chip_dev(x_hi * n_y + owner), device_id_type=MESH,
                     ).start()
 
@@ -373,16 +378,33 @@
     piece_here(3)
     multiply([(0, 0, 8, 0, 2), (1, 0, 5, 0, 2), (1, 5, 8, 0, 1)], False, 3, 4)
     reduce_out(last=True)
-    multiply([(1, 5, 7, 1, 2)], True, 0, 4)
-    reduce_out(last=True)
-    multiply([(1, 7, 8, 1, 2)], True, 0, 4)
-    reduce_out(last=True)
-
-    wait_for(rs_in.at[pl.ds(0, n_y - 1)], rs_recv)
-    for o in range(2):
-        for p in range(2):
-            sum_along_y(o, p)
-        send_along_x(o)
+    multiply([FAR[0]], True, 0, 4)
+    reduce_out(last=True)
+    multiply([FAR[1]], True, 0, 4)
+    reduce_out(last=True)
+
+    distance = lax.rem(y - z + 2 * n_y, n_y)
+    far = jnp.logical_and(distance >= 3, distance <= n_y - 3)
+
+    @pl.when(far)
+    def _():
+        wait_for(rs_in.at[pl.ds(0, n_y - 1), pl.ds(0, 3)], rs_recv.at[0])
+
+    @pl.when(jnp.logical_not(far))
+    def _():
+        wait_for(rs_in.at[pl.ds(0, n_y - 1)], rs_recv.at[0])
+
+    sum_along_y(0, 0)
+    sum_along_y(0, 1)
+    send_along_x(0)
+    sum_along_y(1, 0)
+
+    @pl.when(far)
+    def _():
+        wait_for(rs_in.at[pl.ds(0, n_y - 1), 3], rs_recv.at[1])
+
+    sum_along_y(1, 1)
+    send_along_x(1)
     wait_for(ds_in.at[pl.ds(0, chips - 1)], ds_recv)
     doc_total = jnp.sum(ds_in[...], axis=0)
     here = total[lax.rem(x_hi + col, 2), :, 0:span]
@@ -446,7 +468,7 @@
             pltpu.VMEM((1, docs), F32),
             pltpu.VMEM((chips, 1, docs), F32),
             dma((8 + PIECES,)), dma, dma((2, places, 2, 2)), dma, dma, dma((PIECES,)), dma, dma((64,)),
-            dma, dma, dma, dma((3,)), dma, dma, dma, dma,
+            dma, dma((2,)), dma, dma((3,)), dma, dma, dma, dma,
         ],
         compiler_params=pltpu.CompilerParams(
             collective_id=0, has_side_effects=True, vmem_limit_bytes=63 << 20

time: 82.2 us -> 81.3 us (0.989)
  the two profiles are of different devices: /device:TPU:33 before, /device:TPU:1 now
where the time goes in v4:
time: 81.3 us; the launch traced here: 80 us
  Pallas kernels  78.5 us (97%)
  local copies, waits for them, and re-layouts  1.47 us (2%)
    pallas_call x1, Pallas kernels, shards(): pl.pallas_call(functools.partial(kernel, n_doc, n_layer, swap, factor), o...  78.5 us

profile of v4, /device:TPU:1, one launch (start us, length us, event | category | flops | bytes accessed | tf_op | source)
XLA Modules:
  0.0 80.0 jit_solution(6639267298830496381)
XLA Ops:
  0.0 78.5 %gather_multiply_reduce.1 = f32[32,512]{1,0:T(8,128)} custom-call(bf16[512,4096]{1,0:T(8,128)(2,1)} %bitcast.2, bf16[64,4096]{1,0:T(8,128)(2,1)} %bitcast.3, f32[1,4096]{1,0:T(1,128)} %pc_hbm.1), custom_call_target="tpu_custom_call" | custom-call | flops 4294967296 | bytes 4194304 | tf_op jit(solution)/shard_map/gather_multiply_reduce/pallas_call | solution.py:444
  78.6 1.5 %copy.5 = f32[32,512]{1,0:T(8,128)} copy(f32[32,512]{1,0:T(8,128)} %gather_multiply_reduce.1) | data formatting | bytes 131072

commit v5 on v4

--- a/solution.py
+++ b/solution.py
@@ -338,9 +338,9 @@
                 device_id=(doc, row_dev), device_id_type=MESH,
             ).start()
 
-    doc_squares()
     pass_on(0, 1, 0)
     pass_on(1, 0, 0)
+    doc_squares()
     multiply([(0, 0, 1, 0, 2), (0, 1, 3, 0, 1), (1, 0, 1, 0, 2), (1, 1, 3, 0, 1)], True, 0, 0)
     doc_spread()
     pass_on(0, 2, 0)

time: 81.3 us -> 81.3 us (level)
  no operation moved by 1% of the time
where the time goes in v5:
time: 81.3 us; the launch traced here: 80 us
  Pallas kernels  78.5 us (97%)
  local copies, waits for them, and re-layouts  1.47 us (2%)
    pallas_call x1, Pallas kernels, shards(): pl.pallas_call(functools.partial(kernel, n_doc, n_layer, swap, factor), o...  78.5 us

profile of v5, /device:TPU:1, one launch (start us, length us, event | category | flops | bytes accessed | tf_op | source)
XLA Modules:
  0.0 80.0 jit_solution(17430327669606638555)
XLA Ops:
  0.0 78.5 %gather_multiply_reduce.1 = f32[32,512]{1,0:T(8,128)} custom-call(bf16[512,4096]{1,0:T(8,128)(2,1)} %bitcast.2, bf16[64,4096]{1,0:T(8,128)(2,1)} %bitcast.3, f32[1,4096]{1,0:T(1,128)} %pc_hbm.1), custom_call_target="tpu_custom_call" | custom-call | flops 4294967296 | bytes 4194304 | tf_op jit(solution)/shard_map/gather_multiply_reduce/pallas_call | solution.py:444
  78.6 1.5 %copy.5 = f32[32,512]{1,0:T(8,128)} copy(f32[32,512]{1,0:T(8,128)} %gather_multiply_reduce.1) | data formatting | bytes 131072
